TPU v7x, 32 devices: a whole 2x2x4 slice. The times are simulated.
32 devices in a mesh: dp: 16 (over z, x, core), group: 2 (over y).
Axes of the slice: x: 2, y: 2, z: 4, core: 2. Of those that a mesh axis runs over, the one named last changes fastest.
Arguments:
- queries: bfloat16 [4096, 256], P('dp'), may hold values from -110 to 110
- item_features: bfloat16 [4096, 2048], P('dp', 'group'), may hold values from -6 to 6
- corpus: bfloat16 [32768, 2048], P('dp', 'group'), may hold values from -6 to 6
- sample_ids: int32 [16384], P('dp'), may hold values from 0 to 2047
- sample_shift: bfloat16 [16384], P('dp'), may hold values from -2 to 2
- w1: bfloat16 [2048, 1024], P(None, 'group'), may hold values from -0.125 to 0.125
- w2: bfloat16 [1024, 256], P('group'), may hold values from -0.1875 to 0.1875
Outputs:
- query_loss: float32 [4096], P(('dp', 'group'))
- grad_query: float32 [4096, 256], P(('dp', 'group'))
- grad_w1: float32 [2048, 1024], P(None, 'group')
- grad_w2: float32 [1024, 256], P('group')
Inputs may be any that keep to these rules, and one draw needn't show every extreme that they name: sample_ids[k] is a row of the corpus block of the dp index that holds position k.
All inputs are finite; a program needn't handle non-finite values.
Results may differ from a plain program's by a relative error of at most 0.02.
The roundings to bfloat16 on the way count: a program that leaves them out, or rounds other values in their place, can miss the bound.
Values may be sent and summed in bfloat16 or wider, within the bound.
A program may use at most 128 MiB of HBM per device.

v0:
```python
import jax
import jax.numpy as jnp
from jax import lax
from jax.sharding import PartitionSpec as P


def alternate(head_part, tail_part, groups):
    emb_cols = head_part.shape[1]
    joined = jnp.concatenate(
        [head_part.reshape(groups, -1, emb_cols), tail_part.reshape(groups, -1, emb_cols)], 1
    )
    return joined.reshape(-1, emb_cols)


def per_device(queries, item_features, corpus, sample_ids, sample_shift, w1, w2):
    groups = lax.axis_size("group")
    member = lax.axis_index("group")
    query_rows, emb_width = queries.shape
    quota_rows = query_rows // groups
    neg_rows = sample_ids.shape[0] // groups
    score_scale = emb_width ** (-0.5)
    block_rows = 256
    steps_count = query_rows // block_rows
    picked = jnp.take(corpus, sample_ids, axis=0)
    features_local = alternate(item_features, picked, groups)
    gathered = lax.all_gather(features_local, "group", axis=1, tiled=True)
    pre_act = jnp.dot(gathered, w1, preferred_element_type=jnp.float32)
    hidden = jnp.maximum(pre_act, 0.0).astype(jnp.bfloat16)
    partial_embed = jnp.dot(hidden, w2, preferred_element_type=jnp.float32)
    embedded = lax.psum_scatter(partial_embed, "group", scatter_dimension=0, tiled=True)
    inverse = lax.rsqrt(jnp.mean(embedded * embedded, -1, keepdims=True) + 1e-06)
    normed = (embedded * inverse).astype(jnp.bfloat16)
    shift_own = lax.dynamic_slice_in_dim(sample_shift, member * neg_rows, neg_rows)
    bias_own = jnp.concatenate([jnp.zeros((quota_rows,), jnp.bfloat16), -shift_own])
    stashed, bias_all = (
        lax.all_gather(normed, "dp", axis=0, tiled=True),
        lax.all_gather(bias_own, "dp", axis=0, tiled=True),
    )
    bias_wide = bias_all.astype(jnp.float32)
    query_blocks = queries.reshape(steps_count, block_rows, emb_width)

    def score_block(query_blk):
        return (
            score_scale
            * jnp.einsum("qe,ce->qc", query_blk, stashed, preferred_element_type=jnp.float32)
            + bias_wide
        )

    def row_stats(query_blk):
        logits = score_block(query_blk)
        highest = jnp.max(logits, -1)
        return (highest, jnp.sum(jnp.exp(logits - highest[:, None]), -1))

    highest, row_sum = lax.map(row_stats, query_blocks)
    highest = highest.reshape(query_rows)
    row_sum = row_sum.reshape(query_rows)
    largest = lax.pmax(highest, "group")
    row_sum = lax.psum(row_sum * jnp.exp(highest - largest), "group")
    highest = largest
    log_total = highest + jnp.log(row_sum)
    query_own = lax.dynamic_slice_in_dim(queries, member * quota_rows, quota_rows)
    positive_own = normed[:quota_rows].astype(jnp.float32)
    positive = score_scale * jnp.sum(query_own.astype(jnp.float32) * positive_own, -1)
    query_loss = lax.dynamic_slice_in_dim(log_total, member * quota_rows, quota_rows) - positive
    total_blocks = log_total.reshape(steps_count, block_rows)

    def softmax_block(query_blk, total_blk):
        return jnp.exp(score_block(query_blk) - total_blk[:, None]).astype(jnp.bfloat16)

    def accumulate(grad_acc, inputs):
        query_blk, total_blk = inputs
        softmax = softmax_block(query_blk, total_blk)
        grad_acc = grad_acc + jnp.einsum(
            "qc,qe->ce", softmax, query_blk, preferred_element_type=jnp.float32
        )
        return (grad_acc, jnp.dot(softmax, stashed, preferred_element_type=jnp.float32))

    grad_acc, grad_blocks = lax.scan(
        accumulate, jnp.zeros(stashed.shape, jnp.float32), (query_blocks, total_blocks)
    )
    grad_hat = lax.psum_scatter(grad_acc, "dp", scatter_dimension=0, tiled=True)
    query_sum = lax.psum_scatter(
        grad_blocks.reshape(query_rows, emb_width), "group", scatter_dimension=0, tiled=True
    )
    grad_query = score_scale * (query_sum - positive_own)
    target = jnp.concatenate(
        [query_own.astype(jnp.float32), jnp.zeros((neg_rows, emb_width), jnp.float32)], 0
    )
    grad_normed = score_scale * (grad_hat - target)
    along = jnp.sum(grad_normed * embedded, -1, keepdims=True)
    grad_embed = inverse * grad_normed - inverse**3 * embedded * along / emb_width
    grad_back = lax.all_gather(grad_embed.astype(jnp.bfloat16), "group", axis=0, tiled=True)
    grad_pre = jnp.where(
        pre_act > 0, jnp.dot(grad_back, w2.T, preferred_element_type=jnp.float32), 0.0
    ).astype(jnp.bfloat16)
    grad_w2 = jnp.einsum("rh,re->he", hidden, grad_back, preferred_element_type=jnp.float32)
    grad_w1 = jnp.einsum("rf,rh->fh", gathered, grad_pre, preferred_element_type=jnp.float32)
    grad_w1, grad_w2 = lax.psum((grad_w1, grad_w2), "dp")
    return (query_loss, grad_query, grad_w1, grad_w2)


def solution(mesh):
    in_specs = (
        P("dp", None),
        P("dp", "group"),
        P("dp", "group"),
        P("dp"),
        P("dp"),
        P(None, "group"),
        P("group", None),
    )
    out_specs = (P(("dp", "group")), P(("dp", "group"), None), P(None, "group"), P("group", None))
    return jax.shard_map(
        per_device, mesh=mesh, in_specs=in_specs, out_specs=out_specs, check_vma=False
    )
```

profile of v0, /device:TPU:0, one launch (start us, length us, event | category | flops | bytes accessed | tf_op | source)
XLA Modules:
  0.0 489.6 jit_solution(1353273792064433591)
XLA Ops:
  7.2 0.8 fusion.9
  8.1 0.7 compare_and_fusion
  8.8 8.7 %gather_fusion = bf16[1024,1024]{1,0:T(8,128)(2,1)} fusion(bf16[2048,1024]{1,0:T(8,128)(2,1)} %param.9, s32[1024]{0:T(1024)S(1)} %fusion.9), kind=kCustom, calls=%fused_computation | custom fusion | bytes 4198400 | tf_op jit(solution)/shard_map/jit(_take)/gather | solution.py:24
  17.5 1.9 broadcast_select_fusion
  19.4 1.7 pad_maximum_fusion
  21.2 71.4 %all-gather.4.cloned.1.call-done = bf16[1280,2048]{1,0:T(8,128)(2,1)} async-done(((bf16[1280,1024]{1,0:T(8,128)(2,1)}), bf16[1280,2048]{1,0:T(8,128)(2,1)}) %all-gather.4.cloned.1.call-update) | async-done | bytes 5242896 | tf_op jit(solution)/shard_map/all_gather | solution.py:26
  92.6 4.8 fusion.14
  97.4 1.5 copy-done.2
  98.9 1.6 fusion.6
  100.5 23.3 %reduce-scatter.4.cloned.1.call-done = f32[640,256]{1,0:T(8,128)} async-done(((f32[1280,256]{1,0:T(8,128)}), f32[640,256]{1,0:T(8,128)}) %reduce-scatter.4.cloned.1.call-update) | async-done | bytes 655376 | tf_op jit(solution)/shard_map/reduce_scatter | solution.py:30
  123.8 1.3 multiply_reduce_fusion.1
  125.1 2.0 multiply_convert_fusion
  127.2 0.1 dynamic-slice_negate_fusion
  127.2 21.6 %all-gather = bf16[16,1,640]{2,1,0:T(2,128)(2,1)S(1)} all-gather(bf16[1,1,640]{2,1,0:T(2,128)(2,1)S(1)} %reshape.68), channel_id=1, replica_groups=mesh['dp'=16,'group'=2] {'dp'}, dimensions={0}, use_global_device_ids=true | all-gather | bytes 21760 | tf_op jit(solution)/shard_map/all_gather | solution.py:37
  148.8 34.4 %all-gather.6.cloned.1.call-done = bf16[10240,256]{1,0:T(8,128)(2,1)} async-done(((bf16[640,256]{1,0:T(8,128)(2,1)}), bf16[10240,256]{1,0:T(8,128)(2,1)}) %all-gather.6.cloned.1.call-update) | async-done | bytes 5242896 | tf_op jit(solution)/shard_map/all_gather | solution.py:36
  183.3 6.6 %fusion.13 = (f32[256]{0:T(256)S(1)}, f32[10240,256]{1,0:T(8,128)}) fusion(f32[10240]{0:T(1024)S(1)} %bitcast.18, bf16[10240,256]{1,0:T(8,128)(2,1)} %all-gather.6.cloned.1.call-done, bf16[256,256]{1,0:T(8,128)(2,1)S(1)} %copy-done.3), kind=kOutput, calls=%fused_computation.38 | convolution fusion | flops 1350041344 | bytes 15901696 | tf_op jit(solution)/shard_map/while/body/eval_jaxpr/qe,ce->qc/dot_general | solution.py:45
  189.9 4.9 %pmax.7 = f32[256]{0:T(256)S(1)} all-reduce(f32[256]{0:T(256)S(1)} %get-tuple-element.43), channel_id=1, replica_groups=mesh['dp'=16,'group'=2] {'group'}, use_global_device_ids=true, to_apply=%region_3.4 | all-reduce | flops 256 | bytes 2048 | tf_op jit(solution)/shard_map/pmax | solution.py:57
  194.8 5.2 %exponential_reduce_fusion = f32[256]{0:T(256)S(1)} fusion(f32[10240,256]{1,0:T(8,128)} %get-tuple-element.44, f32[256]{0:T(256)S(1)} %get-tuple-element.43), kind=kLoop, calls=%fused_computation.4 | loop fusion | flops 5242624 | bytes 10487808 | tf_op jit(solution)/shard_map/while/body/eval_jaxpr/reduce_sum | solution.py:52
  200.0 4.9 %psum.21 = f32[256]{0:T(256)S(1)} all-reduce(f32[256]{0:T(256)S(1)} %exponential_multiply_fusion), channel_id=1, replica_groups=mesh['dp'=16,'group'=2] {'group'}, use_global_device_ids=true, to_apply=%region_5.6 | all-reduce | flops 256 | bytes 2048 | tf_op jit(solution)/shard_map/psum | solution.py:58
  205.0 9.5 %fusion.3 = f32[10240,256]{1,0:T(8,128)} fusion(bf16[256,256]{1,0:T(8,128)(2,1)S(1)} %copy-done.3, f32[10240,256]{1,0:T(8,128)} %get-tuple-element.44, f32[256]{0:T(256)S(1)} %log_add_fusion), kind=kOutput, calls=%fused_computation.11 | convolution fusion | flops 1347420160 | bytes 21103616 | tf_op jit(solution)/shard_map/while/body/eval_jaxpr/qc,qe->ce/dot_general | solution.py:73
  214.6 8.4 %fusion.2 = f32[256,256]{1,0:T(8,128)} fusion(bf16[10240,256]{1,0:T(8,128)(2,1)} %all-gather.6.cloned.1.call-done, f32[10240,256]{1,0:T(8,128)} %get-tuple-element.44, f32[256]{0:T(256)S(1)} %log_add_fusion), kind=kOutput, calls=%fused_computation.10 | convolution fusion | flops 1347420160 | bytes 15991808 | tf_op jit(solution)/shard_map/while/body/eval_jaxpr/dot_general | solution.py:76
  223.1 109.3 %reduce-scatter.8.cloned.1.call-done = f32[640,256]{1,0:T(8,128)} async-done(((f32[10240,256]{1,0:T(8,128)}), f32[640,256]{1,0:T(8,128)}) %reduce-scatter.8.cloned.1.call-update) | async-done | bytes 655376 | tf_op jit(solution)/shard_map/reduce_scatter | solution.py:81
  332.3 1.3 multiply_reduce_fusion
  333.6 1.4 subtract_convert_fusion
  335.0 13.0 %all_gather.15 = bf16[1280,256]{1,0:T(8,128)(2,1)S(1)} all-gather(bf16[640,256]{1,0:T(8,128)(2,1)S(1)} %subtract_convert_fusion), channel_id=1, replica_groups=mesh['dp'=16,'group'=2] {'group'}, dimensions={0}, use_global_device_ids=true | all-gather | bytes 983040 | tf_op jit(solution)/shard_map/all_gather | solution.py:92
  348.0 8.6 %fusion.4 = f32[2048,512]{1,0:T(8,128)} fusion(bf16[1280,2048]{1,0:T(8,128)(2,1)} %all-gather.4.cloned.1.call-done, bf16[1280,256]{1,0:T(8,128)(2,1)S(1)} %all_gather.15, bf16[512,256]{1,0:T(8,128)(2,1)S(1)} %copy-done.6, f32[1280,512]{1,0:T(8,128)} %copy-done.2), kind=kOutput, calls=%fused_computation.12 | convolution fusion | flops 3021864960 | bytes 12976128 | tf_op jit(solution)/shard_map/rf,rh->fh/dot_general | solution.py:97
  356.7 3.1 fusion.5
  359.8 1.6 fusion.8
  361.4 0.6 multiply_subtract_fusion
  362.0 115.3 %all-reduce.5.cloned.1.call-done = (f32[2048,512]{1,0:T(8,128)}, f32[512,256]{1,0:T(8,128)}) async-done(((f32[2048,512]{1,0:T(8,128)}, f32[512,256]{1,0:T(8,128)}), (f32[2048,512]{1,0:T(8,128)}, f32[512,256]{1,0:T(8,128)})) %all-reduce.5.cloned.1.call-update) | async-done | bytes 4718608 | tf_op jit(solution)/shard_map/psum | solution.py:98
  477.2 4.7 copy.13
  481.9 0.8 copy.14
  (36 shorter events, 0.5 us)
Async XLA Ops:
  7.2 85.4 %copy-start = (bf16[2048,512]{1,0:T(8,128)(2,1)S(1)}, bf16[2048,512]{1,0:T(8,128)(2,1)}, u32[]{:S(2)}) copy-start(bf16[2048,512]{1,0:T(8,128)(2,1)} %param.12) | copy-start | bytes 6291460
  7.2 85.4 %all-gather.4.cloned.1.call-start = ((), (), s32[]{:S(2)}) async-start(), calls=%async_computation.3 | async-start | bytes 7864320 | tf_op jit(solution)/shard_map/all_gather | solution.py:26
  17.5 1.9 copy-start.4
  21.2 77.7 %copy-start.6 = (bf16[512,256]{1,0:T(8,128)(2,1)S(1)}, bf16[512,256]{1,0:T(8,128)(2,1)}, u32[]{:S(2)}) copy-start(bf16[512,256]{1,0:T(8,128)(2,1)} %param.13) | copy-start | bytes 786436
  21.2 102.6 %reduce-scatter.4.cloned.1.call-start = ((), (), s32[]{:S(2)}) async-start(), calls=%async_computation.4 | async-start | bytes 1966080 | tf_op jit(solution)/shard_map/reduce_scatter | solution.py:30
  97.4 1.5 copy-start.2
  98.9 28.3 %copy-start.7 = (bf16[1024]{0:T(1024)(128)(2,1)S(1)}, bf16[1024]{0:T(1024)(128)(2,1)}, u32[]{:S(2)}) copy-start(bf16[1024]{0:T(1024)(128)(2,1)} %param.11) | copy-start | bytes 6148
  98.9 84.4 %copy-start.3 = (bf16[256,256]{1,0:T(8,128)(2,1)S(1)}, bf16[256,256]{1,0:T(8,128)(2,1)}, u32[]{:S(2)}) copy-start(bf16[256,256]{1,0:T(8,128)(2,1)} %param.7) | copy-start | bytes 393220
  100.5 82.8 %all-gather.6.cloned.1.call-start = ((), (), s32[]{:S(2)}) async-start(), calls=%async_computation.5 | async-start | bytes 5570560 | tf_op jit(solution)/shard_map/all_gather | solution.py:36
  127.1 205.3 %reduce-scatter.8.cloned.1.call-start = ((), (), s32[]{:S(2)}) async-start(), calls=%async_computation.7 | async-start | bytes 11141120 | tf_op jit(solution)/shard_map/reduce_scatter | solution.py:81
  214.5 145.3 %reduce-scatter.6.cloned.1.call-start = ((), (), s32[]{:S(2)}) async-start(), calls=%async_computation.6 | async-start | bytes 393216 | tf_op jit(solution)/shard_map/reduce_scatter | solution.py:82
  214.6 117.7 %copy-start.1 = (f32[640,256]{1,0:T(8,128)S(1)}, f32[640,256]{1,0:T(8,128)}, u32[]{:S(2)}) copy-start(f32[640,256]{1,0:T(8,128)} %reduce-scatter.4.cloned.1.call-done) | copy-start | bytes 1966084
  223.0 254.2 %all-reduce.5.cloned.1.call-start = ((), (), s32[]{:S(2)}) async-start(), calls=%async_computation.8 | async-start | bytes 9437184 | tf_op jit(solution)/shard_map/psum | solution.py:98
  477.2 4.7 copy-start.5
Sparse Core Ops, SparseCore 0:
  21.3 71.2 all-gather.3
  100.6 23.1 reduce-scatter.3
  127.2 56.0 all-gather.5
  214.6 117.6 reduce-scatter.7
  334.5 13.7 reduce-scatter.5
  359.9 117.3 all-reduce.4
where the time goes:
time: 490 us
  waiting for transfers between devices  354 us (72%)
  blocking collectives  44.4 us (9%)
  matrix products  42.6 us (9%)
  other arithmetic  18.6 us (4%)
  local copies, waits for them, and re-layouts  15.8 us (3%)
  between operations  14.2 us (3%)
    psum x1, waiting for transfers between devices, per_device(): grad_w1, grad_w2 = lax.psum((grad_w1, grad_w2), 'dp')  115 us
    reduce_scatter x1, waiting for transfers between devices, per_device(): grad_hat = lax.psum_scatter(grad_acc, 'dp', scatter_dimension=0, tiled=True)  109 us
    all_gather x1, waiting for transfers between devices, per_device(): gathered = lax.all_gather(features_local, 'group', axis=1, tiled=True)  71.4 us
    all_gather x1, waiting for transfers between devices, per_device(): lax.all_gather(normed, 'dp', axis=0, tiled=True)  34.4 us
    reduce_scatter x1, waiting for transfers between devices, per_device(): lax.psum_scatter(partial_embed, 'group', scatter_dimension=0, tiled=True)  23.3 us
    all_gather x1, blocking collectives, per_device(): lax.all_gather(bias_own, 'dp', axis=0, tiled=True)  21.6 us
    all_gather x1, blocking collectives, per_device(): lax.all_gather(grad_embed.astype(jnp.bfloat16), 'group', axis=0, tiled=True)  13 us
  transfers between devices with their start and end apart: 6, of which 5 were waited for; matrix products, arithmetic and copies ran while one was open for 5% of the time, Pallas kernels for 0%

commit v1 on v0

--- a/solution.py
+++ b/solution.py
@@ -2,6 +2,28 @@
 import jax.numpy as jnp
 from jax import lax
 from jax.sharding import PartitionSpec as P
+
+
+def create_the_paths(payload, dim_at):
+    payload = jnp.moveaxis(payload, 0, dim_at)
+    parts_out = payload.shape
+    return payload.reshape(
+        *parts_out[:dim_at], parts_out[dim_at] * parts_out[dim_at + 1], *parts_out[dim_at + 2 :]
+    )
+
+
+def assign_levels_all(content, shard_axis):
+    world_n = lax.axis_size(shard_axis)
+    o_now = content[None]
+    for ii in range(world_n.bit_length() - 1):
+        val2 = 1 << ii
+        tmp = lax.ppermute(
+            o_now, axis_name=shard_axis, perm=[(p, p ^ val2) for p in range(world_n)]
+        )
+        e_now = jnp.stack([o_now, tmp])
+        clean = lax.axis_index(shard_axis) >> ii & 1
+        o_now = jnp.where(clean == 0, e_now, e_now[::-1]).reshape(-1, *content.shape)
+    return o_now
 
 
 def alternate(head_part, tail_part, groups):
@@ -23,7 +45,7 @@
     steps_count = query_rows // block_rows
     picked = jnp.take(corpus, sample_ids, axis=0)
     features_local = alternate(item_features, picked, groups)
-    gathered = lax.all_gather(features_local, "group", axis=1, tiled=True)
+    gathered = create_the_paths(assign_levels_all(features_local, "group"), 1)
     pre_act = jnp.dot(gathered, w1, preferred_element_type=jnp.float32)
     hidden = jnp.maximum(pre_act, 0.0).astype(jnp.bfloat16)
     partial_embed = jnp.dot(hidden, w2, preferred_element_type=jnp.float32)

time: 490 us -> 487 us (level)
  waiting for transfers between devices: 354 us -> 336 us
  local copies, waits for them, and re-layouts: 15.8 us -> 24.6 us
    all_gather x1 -> x0, waiting for transfers between devices: 71.4 us -> none  [per_device(): gathered = lax.all_gather(features_local, 'group', axis=1, tiled=True)]
    ppermute x0 -> x1, waiting for transfers between devices: none -> 52.8 us  [assign_levels_all(): lax.ppermute(o_now, axis_name=shard_axis, perm=[(p, p ^ val2) for p in ra...]
    another operation x0 -> x2, local copies, waits for them, and re-layouts: none -> 8.77 us  [the longest x1 4.39 us: assign_levels_all(): e_now = jnp.stack([o_now, tmp])]
  transfers between devices with their start and end apart: 6 -> 6, of which waited for: 5 -> 5; matrix products, arithmetic and copies ran while one was open for 5% -> 6% of each run, Pallas kernels for 0% -> 0%
where the time goes in v1:
time: 487 us; the launch traced here: 486 us
  waiting for transfers between devices  336 us (69%)
  blocking collectives  44.2 us (9%)
  matrix products  40.8 us (8%)
  local copies, waits for them, and re-layouts  24.6 us (5%)
  other arithmetic  22.6 us (5%)
  between operations  13.9 us (3%)
    psum x1, waiting for transfers between devices, per_device(): grad_w1, grad_w2 = lax.psum((grad_w1, grad_w2), 'dp')  115 us
    reduce_scatter x1, waiting for transfers between devices, per_device(): grad_hat = lax.psum_scatter(grad_acc, 'dp', scatter_dimension=0, tiled=True)  109 us
    ppermute x1, waiting for transfers between devices, assign_levels_all(): lax.ppermute(o_now, axis_name=shard_axis, perm=[(p, p ^ val2) for p in ra...  52.8 us
    all_gather x1, waiting for transfers between devices, per_device(): lax.all_gather(normed, 'dp', axis=0, tiled=True)  34.4 us
    reduce_scatter x1, waiting for transfers between devices, per_device(): lax.psum_scatter(partial_embed, 'group', scatter_dimension=0, tiled=True)  24.8 us
    all_gather x1, blocking collectives, per_device(): lax.all_gather(bias_own, 'dp', axis=0, tiled=True)  21.5 us
    all_gather x1, blocking collectives, per_device(): lax.all_gather(grad_embed.astype(jnp.bfloat16), 'group', axis=0, tiled=True)  12.8 us
  transfers between devices with their start and end apart: 6, of which 5 were waited for; matrix products, arithmetic and copies ran while one was open for 6% of the time, Pallas kernels for 0%

profile of v1, /device:TPU:0, one launch (start us, length us, event | category | flops | bytes accessed | tf_op | source)
XLA Modules:
  0.0 485.9 jit_solution(12874593888362967029)
XLA Ops:
  8.8 8.7 %gather_fusion = bf16[1024,1024]{1,0:T(8,128)(2,1)} fusion(bf16[2048,1024]{1,0:T(8,128)(2,1)} %param.9, s32[1024]{0:T(1024)S(1)} %fusion.9), kind=kCustom, calls=%fused_computation | custom fusion | bytes 4198400 | tf_op jit(solution)/shard_map/jit(_take)/gather | solution.py:46
  17.5 1.9 broadcast_select_fusion
  19.4 1.7 pad_maximum_fusion.1
  21.2 4.4 copy.16
  25.5 3.0 collective-permute-start
  28.5 4.4 copy.15
  32.9 52.8 %collective-permute-done = bf16[1,1280,1024]{1,2,0:T(8,128)(2,1)} collective-permute-done((bf16[1,1280,1024]{1,2,0:T(8,128)(2,1)}, bf16[1,1280,1024]{1,2,0:T(8,128)(2,1)}, u32[]{:S(2)}, u32[]{:S(2)}) %collective-permute-start) | collective-permute-done | bytes 2621472 | tf_op jit(solution)/shard_map/ppermute | solution.py:20
  85.7 3.0 pad_maximum_fusion
  88.7 1.0 reverse_select_fusion
  89.7 2.9 fusion.14
  92.7 1.5 copy-done.3
  94.1 1.6 fusion.6
  95.8 24.8 %reduce-scatter.4.cloned.1.call-done = f32[640,256]{1,0:T(8,128)} async-done(((f32[1280,256]{1,0:T(8,128)}), f32[640,256]{1,0:T(8,128)}) %reduce-scatter.4.cloned.1.call-update) | async-done | bytes 655376 | tf_op jit(solution)/shard_map/reduce_scatter | solution.py:52
  120.6 1.3 multiply_reduce_fusion.1
  121.8 2.0 multiply_convert_fusion
  124.0 21.5 %all-gather = bf16[16,1,640]{2,1,0:T(2,128)(2,1)S(1)} all-gather(bf16[1,1,640]{2,1,0:T(2,128)(2,1)S(1)} %reshape.72), channel_id=1, replica_groups=mesh['dp'=16,'group'=2] {'dp'}, dimensions={0}, use_global_device_ids=true | all-gather | bytes 21760 | tf_op jit(solution)/shard_map/all_gather | solution.py:59
  145.6 34.4 %all-gather.3.cloned.1.call-done = bf16[10240,256]{1,0:T(8,128)(2,1)} async-done(((bf16[640,256]{1,0:T(8,128)(2,1)}), bf16[10240,256]{1,0:T(8,128)(2,1)}) %all-gather.3.cloned.1.call-update) | async-done | bytes 5242896 | tf_op jit(solution)/shard_map/all_gather | solution.py:58
  180.0 6.6 %fusion.13 = (f32[256]{0:T(256)S(1)}, f32[10240,256]{1,0:T(8,128)}) fusion(f32[10240]{0:T(1024)S(1)} %bitcast.28, bf16[10240,256]{1,0:T(8,128)(2,1)} %all-gather.3.cloned.1.call-done, bf16[256,256]{1,0:T(8,128)(2,1)S(1)} %copy-done.5), kind=kOutput, calls=%fused_computation.40 | convolution fusion | flops 1350041344 | bytes 15901696 | tf_op jit(solution)/shard_map/while/body/eval_jaxpr/qe,ce->qc/dot_general | solution.py:67
  186.7 4.9 %pmax.7 = f32[256]{0:T(256)S(1)} all-reduce(f32[256]{0:T(256)S(1)} %get-tuple-element.43), channel_id=1, replica_groups=mesh['dp'=16,'group'=2] {'group'}, use_global_device_ids=true, to_apply=%region_3.4 | all-reduce | flops 256 | bytes 2048 | tf_op jit(solution)/shard_map/pmax | solution.py:79
  191.6 5.2 %exponential_reduce_fusion = f32[256]{0:T(256)S(1)} fusion(f32[10240,256]{1,0:T(8,128)} %get-tuple-element.44, f32[256]{0:T(256)S(1)} %get-tuple-element.43), kind=kLoop, calls=%fused_computation.4 | loop fusion | flops 5242624 | bytes 10487808 | tf_op jit(solution)/shard_map/while/body/eval_jaxpr/reduce_sum | solution.py:74
  196.8 4.9 %psum.21 = f32[256]{0:T(256)S(1)} all-reduce(f32[256]{0:T(256)S(1)} %exponential_multiply_fusion), channel_id=1, replica_groups=mesh['dp'=16,'group'=2] {'group'}, use_global_device_ids=true, to_apply=%region_5.6 | all-reduce | flops 256 | bytes 2048 | tf_op jit(solution)/shard_map/psum | solution.py:80
  201.7 9.5 %fusion.3 = f32[10240,256]{1,0:T(8,128)} fusion(bf16[256,256]{1,0:T(8,128)(2,1)S(1)} %copy-done.5, f32[10240,256]{1,0:T(8,128)} %get-tuple-element.44, f32[256]{0:T(256)S(1)} %log_add_fusion), kind=kOutput, calls=%fused_computation.13 | convolution fusion | flops 1347420160 | bytes 21103616 | tf_op jit(solution)/shard_map/while/body/eval_jaxpr/qc,qe->ce/dot_general | solution.py:95
  211.5 8.4 %fusion.2 = f32[256,256]{1,0:T(8,128)} fusion(bf16[10240,256]{1,0:T(8,128)(2,1)} %all-gather.3.cloned.1.call-done, f32[10240,256]{1,0:T(8,128)} %get-tuple-element.44, f32[256]{0:T(256)S(1)} %log_add_fusion), kind=kOutput, calls=%fused_computation.12 | convolution fusion | flops 1347420160 | bytes 15991808 | tf_op jit(solution)/shard_map/while/body/eval_jaxpr/dot_general | solution.py:98
  220.0 109.0 %reduce-scatter.8.cloned.1.call-done = f32[640,256]{1,0:T(8,128)} async-done(((f32[10240,256]{1,0:T(8,128)}), f32[640,256]{1,0:T(8,128)}) %reduce-scatter.8.cloned.1.call-update) | async-done | bytes 655376 | tf_op jit(solution)/shard_map/reduce_scatter | solution.py:103
  329.0 1.3 multiply_reduce_fusion
  330.3 1.4 subtract_convert_fusion
  331.7 12.8 %all_gather.11 = bf16[1280,256]{1,0:T(8,128)(2,1)S(1)} all-gather(bf16[640,256]{1,0:T(8,128)(2,1)S(1)} %subtract_convert_fusion), channel_id=1, replica_groups=mesh['dp'=16,'group'=2] {'group'}, dimensions={0}, use_global_device_ids=true | all-gather | bytes 983040 | tf_op jit(solution)/shard_map/all_gather | solution.py:114
  344.5 8.6 %fusion.4 = f32[2048,512]{1,0:T(8,128)} fusion(bf16[1280,2048]{0,1:T(8,128)(2,1)} %bitcast.26, bf16[1280,256]{1,0:T(8,128)(2,1)S(1)} %all_gather.11, bf16[512,256]{1,0:T(8,128)(2,1)S(1)} %copy-done.8, f32[1280,512]{1,0:T(8,128)} %copy-done.3), kind=kOutput, calls=%fused_computation.14 | convolution fusion | flops 3021864960 | bytes 12976128 | tf_op jit(solution)/shard_map/rf,rh->fh/dot_general | solution.py:119
  353.2 3.1 fusion.5
  356.3 1.6 fusion.8
  358.5 115.3 %all-reduce.5.cloned.1.call-done = (f32[2048,512]{1,0:T(8,128)}, f32[512,256]{1,0:T(8,128)}) async-done(((f32[2048,512]{1,0:T(8,128)}, f32[512,256]{1,0:T(8,128)}), (f32[2048,512]{1,0:T(8,128)}, f32[512,256]{1,0:T(8,128)})) %all-reduce.5.cloned.1.call-update) | async-done | bytes 4718608 | tf_op jit(solution)/shard_map/psum | solution.py:120
  473.8 4.8 copy.19
  (43 shorter events, 3.6 us)
Async XLA Ops:
  7.2 82.5 %copy-start = (bf16[2048,512]{1,0:T(8,128)(2,1)S(1)}, bf16[2048,512]{1,0:T(8,128)(2,1)}, u32[]{:S(2)}) copy-start(bf16[2048,512]{1,0:T(8,128)(2,1)} %param.12) | copy-start | bytes 6291460
  7.2 113.4 %reduce-scatter.4.cloned.1.call-start = ((), (), s32[]{:S(2)}) async-start(), calls=%async_computation.3 | async-start | bytes 1966080 | tf_op jit(solution)/shard_map/reduce_scatter | solution.py:52
  17.5 1.9 copy-start.6
  25.5 60.1 %collective-permute-start = (bf16[1,1280,1024]{1,2,0:T(8,128)(2,1)}, bf16[1,1280,1024]{1,2,0:T(8,128)(2,1)}, u32[]{:S(2)}, u32[]{:S(2)}) collective-permute-start(bf16[1,1280,1024]{1,2,0:T(8,128)(2,1)} %copy.16), channel_id=1, source_target_pairs={{0,1},{1,0},{2,3},{3,2},{4,5},{5,4},{6,7},{7,6},{8,9},{9,8},{10,11... | collective-permute-start | bytes 7864328 | tf_op jit(solution)/shard_map/ppermute | solution.py:20
  89.7 3.0 copy-start.4
  89.7 4.4 copy-start.8
  92.7 1.5 copy-start.3
  94.1 29.7 %copy-start.9 = (bf16[1024]{0:T(1024)(128)(2,1)S(1)}, bf16[1024]{0:T(1024)(128)(2,1)}, u32[]{:S(2)}) copy-start(bf16[1024]{0:T(1024)(128)(2,1)} %param.11) | copy-start | bytes 6148
  94.1 85.9 %copy-start.5 = (bf16[256,256]{1,0:T(8,128)(2,1)S(1)}, bf16[256,256]{1,0:T(8,128)(2,1)}, u32[]{:S(2)}) copy-start(bf16[256,256]{1,0:T(8,128)(2,1)} %param.7) | copy-start | bytes 393220
  95.7 84.3 %all-gather.3.cloned.1.call-start = ((), (), s32[]{:S(2)}) async-start(), calls=%async_computation.4 | async-start | bytes 5570560 | tf_op jit(solution)/shard_map/all_gather | solution.py:58
  123.8 205.2 %reduce-scatter.8.cloned.1.call-start = ((), (), s32[]{:S(2)}) async-start(), calls=%async_computation.6 | async-start | bytes 11141120 | tf_op jit(solution)/shard_map/reduce_scatter | solution.py:103
  211.2 145.1 %reduce-scatter.6.cloned.1.call-start = ((), (), s32[]{:S(2)}) async-start(), calls=%async_computation.5 | async-start | bytes 393216 | tf_op jit(solution)/shard_map/reduce_scatter | solution.py:104
  211.5 117.5 %copy-start.2 = (f32[640,256]{1,0:T(8,128)S(1)}, f32[640,256]{1,0:T(8,128)}, u32[]{:S(2)}) copy-start(f32[640,256]{1,0:T(8,128)} %reduce-scatter.4.cloned.1.call-done) | copy-start | bytes 1966084
  219.9 253.8 %all-reduce.5.cloned.1.call-start = ((), (), s32[]{:S(2)}) async-start(), calls=%async_computation.7 | async-start | bytes 9437184 | tf_op jit(solution)/shard_map/psum | solution.py:120
  473.8 5.6 %copy-start.1 = (bf16[2048,512]{1,0:T(8,128)(2,1)S(1)}, bf16[2048,512]{1,0:T(8,128)(2,1)}, u32[]{:S(2)}) copy-start(bf16[2048,512]{1,0:T(8,128)(2,1)} %param.12) | copy-start | bytes 6291460
  473.8 4.8 copy-start.7
Sparse Core Ops, SparseCore 0:
  95.8 24.6 reduce-scatter.3
  123.9 56.0 all-gather.2
  211.4 117.6 reduce-scatter.7
  331.2 13.6 reduce-scatter.5
  356.4 117.3 all-reduce.4
